TPU v7x, 32 devices: a whole 2x2x4 slice. The times are simulated.
32 devices in a mesh: modes: 16 (over z, y, x), mom: 2 (over core).
Axes of the slice: x: 2, y: 2, z: 4, core: 2. Of those that a mesh axis runs over, the one named last changes fastest.
Arguments:
- elementals: float32 [2, 4, 256, 256, 256], P(None, 'mom', 'modes'), parts along dimension 1, may hold values from -64 to 64
- perambulators: float32 [16, 2, 2, 256, 256], P('modes'), may hold values from -0.25 to 0.25
- owners: int32 [2], replicated, may hold values from 0 to 15
- pairing: int32 [4], P('mom'), parts along dimension 0, may hold values from 0 to 1
Outputs:
- propagated: bfloat16 [2, 4, 2, 256, 256, 256], P(None, 'mom', None, 'modes'), parts along dimension 1
- correlator: float32 [2, 4, 2], P(None, 'mom'), parts along dimension 1
There are 2 independent parts, one for each index of `mom`. A program takes and returns all parts, laid end to end along the dimension named above; an argument that names none is the same for every part. Nothing has to cross between parts.
All inputs are finite; a program needn't handle non-finite values.
Results may differ from a plain program's by a relative error of at most 0.001.
Values sent between devices are 32-bit elements; how exact they have to be, the bound alone decides.
A program may use at most 192 MiB of HBM per device.

v0:
```python
import jax
import jax.numpy as jnp
from jax import lax
from jax.sharding import PartitionSpec as P

N = 256


highest = lax.Precision.HIGHEST


def spread(block, axis, source):
    block = jnp.where(lax.axis_index(axis) == source, block, jnp.zeros_like(block))
    return lax.psum(block, axis)


def complex_product(formula, matrix_re, matrix_im, tensor_re, tensor_im):

    def single(left_part, right_part):
        return jnp.einsum(formula, left_part, right_part, precision=highest)

    real_part = single(matrix_re, tensor_re) - single(matrix_im, tensor_im)
    imag_part = single(matrix_re, tensor_im) + single(matrix_im, tensor_re)
    return (real_part, imag_part)


def local_pair(elem_re, elem_im, peram_re, peram_im):
    third_re, third_im = complex_product("kc,abc->abk", peram_re, peram_im, elem_re, elem_im)
    result = complex_product("jb,abk->kaj", peram_re, peram_im, third_re, third_im)
    return result


def shards(elementals, perambulators, owners, pairing):
    mom_count = elementals.shape[1]
    time_count = perambulators.shape[1]
    norm_scale = float(N) ** (-1.5)
    perams = []
    for time_index in range(time_count):
        perams.append(spread(perambulators[0, time_index], "modes", owners[time_index]))
    sink_slabs = []
    for mom_index in range(mom_count):
        picked = lax.dynamic_index_in_dim(elementals, pairing[mom_index], 1, keepdims=False)
        sink_slabs.append((jnp.swapaxes(picked[0], 1, 2), jnp.swapaxes(picked[1], 1, 2)))
    carried_re = [[None] * time_count for mom_index in range(mom_count)]
    carried_im = [[None] * time_count for mom_index in range(mom_count)]
    sums_real = [[None] * time_count for mom_index in range(mom_count)]
    sums_imag = [[None] * time_count for mom_index in range(mom_count)]
    for time_index in range(time_count):
        peram_re = perams[time_index][0]
        peram_im = perams[time_index][1]
        outputs = []
        for mom_index in range(mom_count):
            slab_re, slab_im = local_pair(
                elementals[0, mom_index], elementals[1, mom_index], peram_re, peram_im
            )
            outputs.append(
                complex_product(
                    "ia,kaj->kij",
                    peram_re,
                    peram_im,
                    lax.all_to_all(slab_re, "modes", split_axis=0, concat_axis=1, tiled=True),
                    lax.all_to_all(slab_im, "modes", split_axis=0, concat_axis=1, tiled=True),
                )
            )
        for mom_index in range(mom_count):
            out_re, out_im = outputs[mom_index]
            sink_re, sink_im = sink_slabs[mom_index]
            sums_real[mom_index][time_index] = jnp.sum(sink_re * out_re + sink_im * out_im)
            sums_imag[mom_index][time_index] = jnp.sum(sink_re * out_im - sink_im * out_re)
            carried_re[mom_index][time_index] = out_re
            carried_im[mom_index][time_index] = out_im
    partial_sums = jnp.stack(
        [
            jnp.stack([jnp.stack(row) for row in sums_real]),
            jnp.stack([jnp.stack(row) for row in sums_imag]),
        ]
    )
    correlator = lax.psum(partial_sums, "modes") * norm_scale
    propagated = jnp.stack(
        [
            jnp.stack([jnp.stack(row) for row in carried_re]),
            jnp.stack([jnp.stack(row) for row in carried_im]),
        ]
    ).astype(jnp.bfloat16)
    return (propagated, correlator)


def solution(mesh):
    placed = (
        P(None, "mom", "modes", None, None),
        P("modes", None, None, None, None),
        P(),
        P("mom"),
    )
    return jax.shard_map(
        shards,
        mesh=mesh,
        in_specs=placed,
        out_specs=(P(None, "mom", None, "modes", None, None), P(None, "mom", None)),
        check_vma=False,
    )
```

profile of v0, /device:TPU:0, one launch (start us, length us, event | category | flops | bytes accessed | tf_op | source)
XLA Modules:
  0.0 1150.1 jit_solution(14505491117935426496)
XLA Ops:
  12.1 116.5 %all-reduce.3.cloned.1.call-done = (f32[2,256,256]{2,1,0:T(8,128)}, f32[2,256,256]{2,1,0:T(8,128)}) async-done(((f32[2,256,256]{2,1,0:T(8,128)}, f32[2,256,256]{2,1,0:T(8,128)}), (f32[2,256,256]{2,1,0:T(8,128)}, f32[2,256,256]{2,1,0:T(8,128)})) %all-reduce.3.cloned.1.call-update) | async-done | bytes 1048592 | tf_op jit(solution)/shard_map/psum | solution.py:14
  128.6 5.6 fusion.18
  134.2 6.4 fusion.16
  155.5 4.4 copy.83
  159.9 4.6 all-to-all-start.6
  164.5 5.5 fusion
  177.9 65.2 %all-to-all-done.6 = f32[256,16,256]{2,1,0:T(8,128)} async-done(((f32[256,16,256]{2,1,0:T(8,128)}), f32[256,16,256]{2,1,0:T(8,128)}, u32[]{:S(2)}, u32[]{:S(2)}) %all-to-all-start.6) | async-done | bytes 4194336 | tf_op jit(solution)/shard_map/all_to_all | solution.py:61
  243.0 19.3 %all-to-all-start.7 = ((f32[256,16,256]{2,1,0:T(8,128)}), f32[256,16,256]{2,1,0:T(8,128)}, u32[]{:S(2)}, u32[]{:S(2)}) async-start(f32[256,16,256]{2,1,0:T(8,128)} %copy.86), calls=%async_computation.7 | async-start | bytes 8388608 | tf_op jit(solution)/shard_map/all_to_all | solution.py:62
  262.3 5.5 fusion.48
  267.8 5.5 fusion.50
  273.3 12.4 %fusion.89 = f32[256,16,256]{2,0,1:T(8,128)} fusion(f32[256,16,256]{2,0,1:T(8,128)S(1)} %fusion.48, f32[2,2,16,256,256]{4,3,2,1,0:T(8,128)} %param.4, f32[2,256,256]{2,1,0:T(8,128)S(1)} %copy-done.2), kind=kOutput, calls=%fused_computation.110 | convolution fusion | flops 3222274048 | bytes 12845056 | tf_op jit(solution)/shard_map/kc,abc->abk/dot_general | solution.py:20
  285.8 5.3 fusion.32
  291.1 5.9 fusion.86
  304.8 35.9 %all-to-all-done.7 = f32[256,16,256]{2,1,0:T(8,128)} async-done(((f32[256,16,256]{2,1,0:T(8,128)}), f32[256,16,256]{2,1,0:T(8,128)}, u32[]{:S(2)}, u32[]{:S(2)}) %all-to-all-start.7) | async-done | bytes 4194336 | tf_op jit(solution)/shard_map/all_to_all | solution.py:62
  340.7 19.4 %all-to-all-start.3 = ((f32[256,16,256]{2,1,0:T(8,128)}), f32[256,16,256]{2,1,0:T(8,128)}, u32[]{:S(2)}, u32[]{:S(2)}) async-start(f32[256,16,256]{2,1,0:T(8,128)} %copy.74), calls=%async_computation.3 | async-start | bytes 8388608 | tf_op jit(solution)/shard_map/all_to_all | solution.py:62
  360.2 5.5 fusion.34
  369.1 4.4 copy.71
  373.6 65.0 %all-to-all-done.3 = f32[256,16,256]{2,1,0:T(8,128)} async-done(((f32[256,16,256]{2,1,0:T(8,128)}), f32[256,16,256]{2,1,0:T(8,128)}, u32[]{:S(2)}, u32[]{:S(2)}) %all-to-all-start.3) | async-done | bytes 4194336 | tf_op jit(solution)/shard_map/all_to_all | solution.py:62
  438.6 19.5 %all-to-all-start.2 = ((f32[256,16,256]{2,1,0:T(8,128)}), f32[256,16,256]{2,1,0:T(8,128)}, u32[]{:S(2)}, u32[]{:S(2)}) async-start(f32[256,16,256]{2,1,0:T(8,128)} %copy.71), calls=%async_computation.2 | async-start | bytes 8388608 | tf_op jit(solution)/shard_map/all_to_all | solution.py:61
  458.1 5.5 fusion.22
  463.6 5.5 fusion.20
  469.1 5.5 fusion.103
  480.1 6.0 fusion.100
  493.9 42.6 %all-to-all-done.2 = f32[256,16,256]{2,1,0:T(8,128)} async-done(((f32[256,16,256]{2,1,0:T(8,128)}), f32[256,16,256]{2,1,0:T(8,128)}, u32[]{:S(2)}, u32[]{:S(2)}) %all-to-all-start.2) | async-done | bytes 4194336 | tf_op jit(solution)/shard_map/all_to_all | solution.py:61
  536.5 19.3 %all-to-all-start.4 = ((f32[256,16,256]{2,1,0:T(8,128)}), f32[256,16,256]{2,1,0:T(8,128)}, u32[]{:S(2)}, u32[]{:S(2)}) async-start(f32[256,16,256]{2,1,0:T(8,128)} %copy.77), calls=%async_computation.4 | async-start | bytes 8388608 | tf_op jit(solution)/shard_map/all_to_all | solution.py:61
  555.8 5.5 fusion.8
  564.7 4.5 copy.80
  569.2 65.0 %all-to-all-done.4 = f32[256,16,256]{2,1,0:T(8,128)} async-done(((f32[256,16,256]{2,1,0:T(8,128)}), f32[256,16,256]{2,1,0:T(8,128)}, u32[]{:S(2)}, u32[]{:S(2)}) %all-to-all-start.4) | async-done | bytes 4194336 | tf_op jit(solution)/shard_map/all_to_all | solution.py:61
  634.2 19.5 %all-to-all-start.5 = ((f32[256,16,256]{2,1,0:T(8,128)}), f32[256,16,256]{2,1,0:T(8,128)}, u32[]{:S(2)}, u32[]{:S(2)}) async-start(f32[256,16,256]{2,1,0:T(8,128)} %copy.80), calls=%async_computation.5 | async-start | bytes 8388608 | tf_op jit(solution)/shard_map/all_to_all | solution.py:62
  653.7 5.5 fusion.52
  659.2 5.5 fusion.54
  664.7 5.5 fusion.83
  675.7 5.7 fusion.80
  684.9 4.4 copy.68
  689.3 42.8 %all-to-all-done.5 = f32[256,16,256]{2,1,0:T(8,128)} async-done(((f32[256,16,256]{2,1,0:T(8,128)}), f32[256,16,256]{2,1,0:T(8,128)}, u32[]{:S(2)}, u32[]{:S(2)}) %all-to-all-start.5) | async-done | bytes 4194336 | tf_op jit(solution)/shard_map/all_to_all | solution.py:62
  732.1 19.7 %all-to-all-start.1 = ((f32[256,16,256]{2,1,0:T(8,128)}), f32[256,16,256]{2,1,0:T(8,128)}, u32[]{:S(2)}, u32[]{:S(2)}) async-start(f32[256,16,256]{2,1,0:T(8,128)} %copy.68), calls=%async_computation.1 | async-start | bytes 8388608 | tf_op jit(solution)/shard_map/all_to_all | solution.py:62
  751.8 5.5 fusion.42
  760.8 4.5 copy.65
  765.2 65.0 %all-to-all-done.1 = f32[256,16,256]{2,1,0:T(8,128)} async-done(((f32[256,16,256]{2,1,0:T(8,128)}), f32[256,16,256]{2,1,0:T(8,128)}, u32[]{:S(2)}, u32[]{:S(2)}) %all-to-all-start.1) | async-done | bytes 4194336 | tf_op jit(solution)/shard_map/all_to_all | solution.py:62
  830.2 19.4 %all-to-all-start = ((f32[256,16,256]{2,1,0:T(8,128)}), f32[256,16,256]{2,1,0:T(8,128)}, u32[]{:S(2)}, u32[]{:S(2)}) async-start(f32[256,16,256]{2,1,0:T(8,128)} %copy.65), calls=%async_computation | async-start | bytes 8388608 | tf_op jit(solution)/shard_map/all_to_all | solution.py:61
  871.1 4.8 copy.69
  875.9 8.5 fusion.124
  884.4 8.5 fusion.126
  892.9 8.7 fusion.127
  901.6 8.9 fusion.125
  910.5 6.7 fusion.120
  917.2 6.9 fusion.122
  924.1 10.1 convolution_add_fusion
  934.2 10.3 convolution_subtract_fusion
  944.5 8.5 convolution_subtract_fusion.2
  953.0 8.8 convolution_add_fusion.2
  961.8 8.5 convolution_add_fusion.1
  970.3 8.5 convolution_subtract_fusion.1
  981.9 9.0 fusion.123
  990.8 7.0 fusion.121
  997.9 8.7 convolution_add_fusion.3
  1006.7 30.6 %add_reduce_fusion.3 = (f32[]{:T(128)}, f32[]{:T(128)}, f32[]{:T(128)}, f32[]{:T(128)}, f32[]{:T(128)}, /*index=5*/f32[]{:T(128)}, f32[]{:T(128)}, f32[]{:T(128)...) fusion(f32[16,256,256]{2,1,0:T(8,128)} %convolution_add_fusion., ...), kind=kOutput, calls=%fused_computation.82 | convolution fusion | flops 3264217088 | bytes 71565360 | tf_op jit(solution)/shard_map/ia,kaj->kij/dot_general | solution.py:20
  1042.7 42.2 %psum.23 = f32[2,2,2]{2,1,0:T(2,128)S(1)} all-reduce(f32[2,2,2]{2,1,0:T(2,128)S(1)} %pad_maximum_fusion.1), channel_id=1, replica_groups=mesh['modes'=16,'mom'=2] {'modes'}, use_global_device_ids=true, to_apply=%region_10.11 | all-reduce | flops 8 | bytes 64 | tf_op jit(solution)/shard_map/psum | solution.py:78
  1085.4 5.1 maximum_bitcast_fusion.4
  1090.5 6.5 maximum_bitcast_fusion.1
  1097.0 4.5 maximum_bitcast_fusion.2
  1101.5 6.2 maximum_bitcast_fusion
  1107.7 13.8 %pad_maximum_fusion = bf16[2,2,2,16,256,256]{4,5,3,2,1,0:T(8,128)(2,1)} fusion(bf16[1,2,2,16,256,256]{4,5,3,2,1,0:T(8,128)(2,1)} %maximum_bitcast_fusion.1, bf16[1,2,2,16,256,256]{4,5,3,2,1,0:T(8,128)(2,1)} %maximum_bitcast_fusion), kind=kLoop, calls=%fused_computation | loop fusion | flops 8388608 | bytes 33554432 | tf_op jit(solution)/shard_map/stack | solution.py:79
  1121.5 21.5 %copy.97 = bf16[2,2,2,16,256,256]{5,4,3,2,1,0:T(8,128)(2,1)} copy(bf16[2,2,2,16,256,256]{4,5,3,2,1,0:T(8,128)(2,1)} %pad_maximum_fusion) | data formatting | bytes 33554432
  (82 shorter events, 93.1 us)
Async XLA Ops:
  7.2 121.4 %all-reduce.3.cloned.1.call-start = ((), (), s32[]{:S(2)}) async-start(), calls=%async_computation.8 | async-start | bytes 2097152 | tf_op jit(solution)/shard_map/psum | solution.py:14
  128.6 12.1 %copy-start = (f32[2,2,16,256,256]{4,3,2,1,0:T(8,128)S(1)}, f32[2,2,16,256,256]{4,3,2,1,0:T(8,128)}, u32[]{:S(2)}) copy-start(f32[2,2,16,256,256]{4,3,2,1,0:T(8,128)} %param.4) | copy-start | bytes 50331652
  134.2 6.5 copy-start.2
  144.5 7.3 copy-start.9
  148.3 3.5 copy-start.14
  159.9 83.1 %all-to-all-start.6 = ((f32[256,16,256]{2,1,0:T(8,128)}), f32[256,16,256]{2,1,0:T(8,128)}, u32[]{:S(2)}, u32[]{:S(2)}) async-start(f32[256,16,256]{2,1,0:T(8,128)} %copy.83), calls=%async_computation.6 | async-start | bytes 8388608 | tf_op jit(solution)/shard_map/all_to_all | solution.py:61
  164.5 5.5 copy-start.10
  243.0 97.7 %all-to-all-start.7 = ((f32[256,16,256]{2,1,0:T(8,128)}), f32[256,16,256]{2,1,0:T(8,128)}, u32[]{:S(2)}, u32[]{:S(2)}) async-start(f32[256,16,256]{2,1,0:T(8,128)} %copy.86), calls=%async_computation.7 | async-start | bytes 8388608 | tf_op jit(solution)/shard_map/all_to_all | solution.py:62
  297.0 3.5 copy-start.3
  340.7 97.9 %all-to-all-start.3 = ((f32[256,16,256]{2,1,0:T(8,128)}), f32[256,16,256]{2,1,0:T(8,128)}, u32[]{:S(2)}, u32[]{:S(2)}) async-start(f32[256,16,256]{2,1,0:T(8,128)} %copy.74), calls=%async_computation.3 | async-start | bytes 8388608 | tf_op jit(solution)/shard_map/all_to_all | solution.py:62
  360.2 5.5 copy-start.4
  373.6 84.5 %copy-start.1 = (f32[2,256,256]{2,1,0:T(8,128)S(1)}, f32[2,256,256]{2,1,0:T(8,128)}, u32[]{:S(2)}) copy-start(f32[2,256,256]{2,1,0:T(8,128)} %get-tuple-element.25) | copy-start | bytes 1572868
  438.6 97.9 %all-to-all-start.2 = ((f32[256,16,256]{2,1,0:T(8,128)}), f32[256,16,256]{2,1,0:T(8,128)}, u32[]{:S(2)}, u32[]{:S(2)}) async-start(f32[256,16,256]{2,1,0:T(8,128)} %copy.71), calls=%async_computation.2 | async-start | bytes 8388608 | tf_op jit(solution)/shard_map/all_to_all | solution.py:61
  474.6 2.0 copy-start.12
  486.1 3.5 copy-start.5
  536.5 97.7 %all-to-all-start.4 = ((f32[256,16,256]{2,1,0:T(8,128)}), f32[256,16,256]{2,1,0:T(8,128)}, u32[]{:S(2)}, u32[]{:S(2)}) async-start(f32[256,16,256]{2,1,0:T(8,128)} %copy.77), calls=%async_computation.4 | async-start | bytes 8388608 | tf_op jit(solution)/shard_map/all_to_all | solution.py:61
  555.8 5.5 copy-start.6
  634.2 97.9 %all-to-all-start.5 = ((f32[256,16,256]{2,1,0:T(8,128)}), f32[256,16,256]{2,1,0:T(8,128)}, u32[]{:S(2)}, u32[]{:S(2)}) async-start(f32[256,16,256]{2,1,0:T(8,128)} %copy.80), calls=%async_computation.5 | async-start | bytes 8388608 | tf_op jit(solution)/shard_map/all_to_all | solution.py:62
  670.2 1.9 copy-start.13
  681.4 3.5 copy-start.7
  732.1 98.1 %all-to-all-start.1 = ((f32[256,16,256]{2,1,0:T(8,128)}), f32[256,16,256]{2,1,0:T(8,128)}, u32[]{:S(2)}, u32[]{:S(2)}) async-start(f32[256,16,256]{2,1,0:T(8,128)} %copy.68), calls=%async_computation.1 | async-start | bytes 8388608 | tf_op jit(solution)/shard_map/all_to_all | solution.py:62
  751.8 5.5 copy-start.8
  765.2 84.5 %copy-start.18 = (s32[2]{0:T(128)S(1)}, s32[2]{0:T(128)}, u32[]{:S(2)}) copy-start(s32[2]{0:T(128)} %param.7) | copy-start | bytes 28
  830.2 148.6 %all-to-all-start = ((f32[256,16,256]{2,1,0:T(8,128)}), f32[256,16,256]{2,1,0:T(8,128)}, u32[]{:S(2)}, u32[]{:S(2)}) async-start(f32[256,16,256]{2,1,0:T(8,128)} %copy.65), calls=%async_computation | async-start | bytes 8388608 | tf_op jit(solution)/shard_map/all_to_all | solution.py:61
  934.2 10.3 copy-start.16
  944.5 8.5 copy-start.15
  978.9 27.8 %slice-start = ((s8[16777216]{0:T(1024)(128)(4,1)}), s8[4194304]{0:T(1024)(128)(4,1)S(1)}, s32[]{:S(2)}) async-start(s8[16777216]{0:T(1024)(128)(4,1)} %bitcast.346), calls=%async_computation.9 | async-start | bytes 8388608
  981.9 9.0 copy-start.11
  981.9 24.8 %slice-start.1 = ((s8[16777216]{0:T(1024)(128)(4,1)}), s8[4194304]{0:T(1024)(128)(4,1)S(1)}, s32[]{:S(2)}) async-start(s8[16777216]{0:T(1024)(128)(4,1)} %bitcast.346), calls=%async_computation.10 | async-start | bytes 8388608
  990.8 15.8 %slice-start.2 = ((s8[16777216]{0:T(1024)(128)(4,1)}), s8[4194304]{0:T(1024)(128)(4,1)S(1)}, s32[]{:S(2)}) async-start(s8[16777216]{0:T(1024)(128)(4,1)} %bitcast.346), calls=%async_computation.11 | async-start | bytes 8388608
  997.9 8.8 slice-start.3
  1090.5 6.5 copy-start.17
Sparse Core Ops, SparseCore 0:
  13.9 114.6 all-reduce.2
where the time goes:
time: 1160 us; the launch traced here: 1150 us
  waiting for transfers between devices  498 us (43%)
  matrix products  317 us (27%)
  starting transfers between devices  141 us (12%)
  local copies, waits for them, and re-layouts  87.5 us (8%)
  other arithmetic  44.3 us (4%)
  blocking collectives  42.2 us (4%)
  between operations  20.1 us (2%)
    dot_general x48, matrix products, single(): return jnp.einsum(formula, left_part, right_part, precision=highest)  317 us
    all_to_all x4, waiting for transfers between devices, shards(): lax.all_to_all(slab_im, 'modes', split_axis=0, concat_axis=1, tiled=True)  209 us
    all_to_all x4, waiting for transfers between devices, shards(): lax.all_to_all(slab_re, 'modes', split_axis=0, concat_axis=1, tiled=True)  173 us
    psum x1, waiting for transfers between devices, spread(): return lax.psum(block, axis)  116 us
    all_to_all x4, starting transfers between devices, shards(): lax.all_to_all(slab_im, 'modes', split_axis=0, concat_axis=1, tiled=True)  77.9 us
    all_to_all x4, starting transfers between devices, shards(): lax.all_to_all(slab_re, 'modes', split_axis=0, concat_axis=1, tiled=True)  62.7 us
    psum x1, blocking collectives, shards(): correlator = lax.psum(partial_sums, 'modes') * norm_scale  42.2 us
    another operation x3, other arithmetic, shards(): jnp.stack([jnp.stack([jnp.stack(row) for row in carried_re]), jnp.stack([...  26.5 us
  transfers between devices with their start and end apart: 9, of which 8 were waited for; matrix products, arithmetic and copies ran while one was open for 25% of the time, Pallas kernels for 0%

commit v1 on v0

v1 whole, which is shorter than its diff:
```python
import jax
import jax.numpy as jnp
from jax import lax
from jax.sharding import PartitionSpec as P

high = lax.Precision.HIGH


def scatter_pick_gather(perams, owners, mode_count, mom_count):
    times, parts, n = perams.shape[0], perams.shape[1], perams.shape[2]
    rows = parts * n
    both = rows % (8 * mode_count * mom_count) == 0
    pieces = mode_count * mom_count if both else mode_count
    names = ("modes", "mom") if both else "modes"
    flat = jnp.swapaxes(perams.reshape(times, pieces, rows // pieces, n), 0, 1)
    if both:
        flat = flat.reshape((mode_count, mom_count) + flat.shape[1:])
        flat = lax.dynamic_index_in_dim(flat, lax.axis_index("mom"), 1, keepdims=False)
    seen = lax.all_to_all(flat, "modes", split_axis=0, concat_axis=0, tiled=True)
    mine = jnp.stack(
        [lax.dynamic_index_in_dim(seen[:, t], owners[t], 0, keepdims=False) for t in range(times)]
    )
    spread_out = jnp.broadcast_to(mine[None], (pieces,) + mine.shape)
    whole = lax.all_to_all(spread_out, names, split_axis=0, concat_axis=0, tiled=True)
    return jnp.swapaxes(whole, 0, 1).reshape(times, parts, n, n)


def real_form(peram):
    re, im = peram[0], peram[1]
    return jnp.stack([jnp.stack([re, -im], axis=1), jnp.stack([im, re], axis=1)])


def before(elem, form, mode_count):
    third = jnp.einsum("PkCc,Cabc->Pabk", form, elem, precision=high)
    second = jnp.einsum("QjPb,Pabk->Qkaj", form, third, precision=high)
    comps, n, slab, _ = second.shape
    return jnp.moveaxis(second.reshape(comps, mode_count, n // mode_count, slab, n), 1, 0)


def after(arrived, form, mode_count):
    comps, n = form.shape[0], form.shape[1]
    split = form.reshape(comps, n, comps, mode_count, n // mode_count)
    return jnp.einsum("RiQsa,sQkaj->Rkij", split, arrived, precision=high)


def shards(mode_count, mom_count, elementals, perambulators, owners, pairing):
    momenta = elementals.shape[1]
    times = perambulators.shape[1]
    n = elementals.shape[-1]
    norm_scale = float(n) ** (-1.5)
    taus = scatter_pick_gather(perambulators[0], owners, mode_count, mom_count)
    forms = [real_form(taus[t]) for t in range(times)]
    steps = [(t, m) for t in range(times) for m in range(momenta)]
    slab = elementals.shape[2]
    out = jnp.zeros((2, momenta, times, slab, n, n), jnp.bfloat16)
    sums = {}

    def finish(step, arrived, out):
        t, m = step
        result = after(arrived, forms[t], mode_count)
        rounded = result.astype(jnp.bfloat16)[:, None, None]
        out = lax.dynamic_update_slice(out, rounded, (0, m, t, 0, 0, 0))
        sink = lax.dynamic_index_in_dim(elementals, pairing[m], 1, keepdims=False)
        sink = jnp.swapaxes(sink, 2, 3)
        real = jnp.sum(sink[0] * result[0] + sink[1] * result[1])
        imag = jnp.sum(sink[0] * result[1] - sink[1] * result[0])
        sums[step] = (real, imag)
        return out, real, imag

    waiting = None
    for index, (t, m) in enumerate(steps):
        elem, form = elementals[:, m], forms[t]
        if index >= 2:
            (out, real, imag), form = lax.optimization_barrier(
                (finish(steps[index - 2], waiting[index - 2], out), form)
            )
            sums[steps[index - 2]] = (real, imag)
        else:
            waiting = waiting or {}
        packed = before(elem, form, mode_count)
        waiting[index] = lax.all_to_all(packed, "modes", split_axis=0, concat_axis=0, tiled=True)
    for index in range(max(len(steps) - 2, 0), len(steps)):
        out, real, imag = finish(steps[index], waiting[index], out)

    partial = jnp.stack(
        [
            jnp.stack([jnp.stack([sums[(t, m)][c] for t in range(times)]) for m in range(momenta)])
            for c in range(2)
        ]
    )
    shares = jnp.broadcast_to(partial.reshape(1, 1, -1), (mode_count, 1, partial.size))
    shares = lax.all_to_all(shares, "modes", split_axis=0, concat_axis=0, tiled=True)
    correlator = jnp.sum(shares, axis=(0, 1)).reshape(partial.shape) * norm_scale
    return (out, correlator)


def solution(mesh):
    mode_count, mom_count = mesh.shape["modes"], mesh.shape["mom"]
    placed = (
        P(None, "mom", "modes", None, None),
        P("modes", None, None, None, None),
        P(),
        P("mom"),
    )

    def local(elementals, perambulators, owners, pairing):
        return shards(mode_count, mom_count, elementals, perambulators, owners, pairing)

    return jax.shard_map(
        local,
        mesh=mesh,
        in_specs=placed,
        out_specs=(P(None, "mom", None, "modes", None, None), P(None, "mom", None)),
        check_vma=False,
    )
```

time: 1160 us -> 926 us (0.80)
  matrix products: 317 us -> 125 us
  blocking collectives: 42.2 us -> 0 us
  local copies, waits for them, and re-layouts: 87.5 us -> 120 us
  starting transfers between devices: 141 us -> 172 us
  waiting for transfers between devices: 498 us -> 467 us
  other arithmetic: 44.3 us -> 23 us
    dot_general x48 -> x12, matrix products: 317 us -> 125 us  [the longest x4 47.5 us: before(): second = jnp.einsum('QjPb,Pabk->Qkaj', form, third, precision=high)]
    psum x1 -> x0, waiting for transfers between devices: 116 us -> none  [spread(): return lax.psum(block, axis)]
    all_to_all x8 -> x7, waiting for transfers between devices: 381 us -> 467 us  [the longest x4 457 us: shards(): lax.all_to_all(packed, 'modes', split_axis=0, concat_axis=0, tiled=True)]
    psum x1 -> x0, blocking collectives: 42.2 us -> none  [shards(): correlator = lax.psum(partial_sums, 'modes') * norm_scale]
    another operation x10 -> x11, other arithmetic: 41.5 us -> 5.58 us  [the longest x4 5.31 us: shards(): jnp.stack([jnp.stack([sums[t, m][c] for t in range(times)]) for m in rang...]
    dynamic_slice x0 -> x4, local copies, waits for them, and re-layouts: none -> 35.3 us  [the longest x3 35.3 us: finish(): sink = lax.dynamic_index_in_dim(elementals, pairing[m], 1, keepdims=False)]
    all_to_all x8 -> x7, starting transfers between devices: 141 us -> 172 us  [the longest x4 122 us: shards(): lax.all_to_all(packed, 'modes', split_axis=0, concat_axis=0, tiled=True)]
    all_to_all x8 -> x0, local copies, waits for them, and re-layouts: 24.7 us -> none  [the longest x4 13.3 us: shards(): lax.all_to_all(slab_im, 'modes', split_axis=0, concat_axis=1, tiled=True)]
  transfers between devices with their start and end apart: 9 -> 7, of which waited for: 8 -> 5; matrix products, arithmetic and copies ran while one was open for 25% -> 23% of each run, Pallas kernels for 0% -> 0%
where the time goes in v1:
time: 926 us; the launch traced here: 917 us
  waiting for transfers between devices  467 us (50%)
  starting transfers between devices  172 us (19%)
  matrix products  125 us (13%)
  local copies, waits for them, and re-layouts  120 us (13%)
  other arithmetic  23 us (2%)
    all_to_all x4, waiting for transfers between devices, shards(): lax.all_to_all(packed, 'modes', split_axis=0, concat_axis=0, tiled=True)  457 us
    all_to_all x4, starting transfers between devices, shards(): lax.all_to_all(packed, 'modes', split_axis=0, concat_axis=0, tiled=True)  122 us
    dot_general x4, matrix products, before(): second = jnp.einsum('QjPb,Pabk->Qkaj', form, third, precision=high)  47.5 us
    dot_general x4, matrix products, after(): return jnp.einsum('RiQsa,sQkaj->Rkij', split, arrived, precision=high)  43.3 us
    all_to_all x1, starting transfers between devices, shards(): lax.all_to_all(shares, 'modes', split_axis=0, concat_axis=0, tiled=True)  39.1 us
    dynamic_slice x3, local copies, waits for them, and re-layouts, finish(): sink = lax.dynamic_index_in_dim(elementals, pairing[m], 1, keepdims=False)  35.3 us
    dot_general x4, matrix products, before(): third = jnp.einsum('PkCc,Cabc->Pabk', form, elem, precision=high)  34.2 us
    unnamed x33, local copies, waits for them, and re-layouts  31.2 us
  transfers between devices with their start and end apart: 7, of which 5 were waited for; matrix products, arithmetic and copies ran while one was open for 23% of the time, Pallas kernels for 0%

profile of v1, /device:TPU:0, one launch (start us, length us, event | category | flops | bytes accessed | tf_op | source)
XLA Modules:
  0.0 916.9 jit_solution(7497462287194609131)
XLA Ops:
  0.6 1.3 copy.101
  2.0 0.8 dynamic-slice_bitcast_fusion
  2.8 8.3 all-to-all-start
  11.1 1.3 fusion.39
  16.3 10.0 %all-to-all-done = f32[16,2,16,256]{3,2,1,0:T(8,128)S(1)} async-done(((f32[16,2,16,256]{3,2,1,0:T(8,128)}), f32[16,2,16,256]{3,2,1,0:T(8,128)S(1)}, u32[]{:S(2)}, u32[]{:S(2)}) %all-to-all-start) | async-done | bytes 524320 | tf_op jit(solution)/shard_map/all_to_all | solution.py:19
  26.3 1.1 broadcast_in_dim.26
  27.4 2.9 all-to-all-start.1
  34.8 23.8 %constant_dynamic-slice_fusion = (f32[2,1,16,256,256]{4,3,2,1,0:T(8,128)}, f32[2,1,16,256,256]{4,3,2,1,0:T(8,128)}, f32[2,1,16,256,256]{4,3,2,1,0:T(8,128)}, f32[2,1,16,256,256]{4,3,2,1,0:T(8,128)}) fusion(f32[2,2,16,256,256]{4,3,2,1,0:T(8,128)} %param.4, s32[]{:T(128)S(6)} %select_n.24, s32[]{:T(128)S(6)} %select_n.23), kind=kLoop, calls=%fused_computation.61 | loop fusion | bytes 67108872 | tf_op jit(solution)/shard_map/jit(dynamic_index_in_dim)/dynamic_slice | solution.py:63
  58.9 9.5 %fusion.22 = f32[2,16,256,256,1]{2,3,0,1,4:T(8,128)S(1)} fusion(f32[2,1,16,256,256]{4,3,2,1,0:T(8,128)} %get-tuple-element.41, f32[1,256,2,256]{3,1,2,0:T(8,128)S(1)} %get-tuple-element.53, f32[1,256,2,256]{3,1,2,0:T(8,128)S(1)} %get-tuple-element.52), kind=kOutput, calls=%fused_computation.42 | convolution fusion | flops 6442713088 | bytes 17825792 | tf_op jit(solution)/shard_map/PkCc,Cabc->Pabk/dot_general | solution.py:34
  68.4 11.8 %fusion.14 = f32[16,256,2,256,1]{3,0,4,2,1:T(8,128)} fusion(f32[2,16,256,256,1]{2,3,0,1,4:T(8,128)S(1)} %fusion.22, f32[1,256,2,256]{3,1,2,0:T(8,128)S(1)} %get-tuple-element.53, f32[1,256,2,256]{3,1,2,0:T(8,128)S(1)} %get-tuple-element.52), kind=kOutput, calls=%fused_computation.16 | convolution fusion | flops 6442713088 | bytes 17825792 | tf_op jit(solution)/shard_map/QjPb,Pabk->Qkaj/dot_general | solution.py:35
  80.2 7.1 all-to-all-start.2
  87.3 9.5 %fusion.20 = f32[2,16,256,256,1]{2,3,0,1,4:T(8,128)S(1)} fusion(f32[2,1,16,256,256]{4,3,2,1,0:T(8,128)} %get-tuple-element.42, f32[1,256,2,256]{3,1,2,0:T(8,128)S(1)} %get-tuple-element.53, f32[1,256,2,256]{3,1,2,0:T(8,128)S(1)} %get-tuple-element.52), kind=kOutput, calls=%fused_computation.40 | convolution fusion | flops 6442713088 | bytes 17825792 | tf_op jit(solution)/shard_map/PkCc,Cabc->Pabk/dot_general | solution.py:34
  96.8 11.8 %fusion.12 = f32[16,256,2,256,1]{3,0,4,2,1:T(8,128)} fusion(f32[2,16,256,256,1]{2,3,0,1,4:T(8,128)S(1)} %fusion.20, f32[1,256,2,256]{3,1,2,0:T(8,128)S(1)} %get-tuple-element.53, f32[1,256,2,256]{3,1,2,0:T(8,128)S(1)} %get-tuple-element.52), kind=kOutput, calls=%fused_computation.14 | convolution fusion | flops 6442713088 | bytes 17825792 | tf_op jit(solution)/shard_map/QjPb,Pabk->Qkaj/dot_general | solution.py:35
  108.6 137.6 %all-to-all-done.2 = f32[16,2,16,16,256]{4,3,1,2,0:T(8,128)} async-done(((f32[16,2,16,16,256]{4,3,1,2,0:T(8,128)}), f32[16,2,16,16,256]{4,3,1,2,0:T(8,128)}, u32[]{:S(2)}, u32[]{:S(2)}) %all-to-all-start.2) | async-done | bytes 8388640 | tf_op jit(solution)/shard_map/all_to_all | solution.py:81
  246.3 38.1 %all-to-all-start.3 = ((f32[16,2,16,16,256]{4,3,1,2,0:T(8,128)}), f32[16,2,16,16,256]{4,3,1,2,0:T(8,128)}, u32[]{:S(2)}, u32[]{:S(2)}) async-start(f32[16,2,16,16,256]{4,3,1,2,0:T(8,128)} %bitcast.251), calls=%async_computation.3 | async-start | bytes 16777216 | tf_op jit(solution)/shard_map/all_to_all | solution.py:81
  284.3 7.5 copy.196
  291.8 2.1 squeeze.41
  293.9 0.6 stack.122
  294.5 2.5 copy.104
  297.0 0.8 neg.35
  297.8 1.7 copy.105
  299.7 11.1 %fusion.6 = f32[16,256,2,256,1,1]{3,1,4,0,2,5:T(8,128)S(1)} fusion(f32[16,2,16,16,256]{4,3,1,2,0:T(8,128)} %all-to-all-done.2, f32[1,256,1,16,16]{1,4,2,0,3:T(8,128)} %copy.105, f32[1,256,1,16,16]{1,4,2,0,3:T(8,128)} %copy-done.5, f32[1,256,1,16,16]{1,4,2,0,3:T(8,128)} %neg.35), kind=kOutput, calls=%fused_computation.8 | convolution fusion | flops 6443237376 | bytes 17563648 | tf_op jit(solution)/shard_map/RiQsa,sQkaj->Rkij/dot_general | solution.py:43
  310.8 3.2 copy-done.4
  314.1 0.9 copy.194
  315.0 6.2 copy.197
  321.2 9.9 %dynamic_update_slice.12 = bf16[2,2,2,16,256,256]{4,5,0,3,2,1:T(8,128)(2,1)} pad(bf16[2,1,1,16,256,256]{4,5,0,3,2,1:T(8,128)(2,1)} %bitcast.259, bf16[]{:T(256)} %constant.34.clone.1), padding=0_0x0_1x0_1x0_0x0_0x0_0 | pad | bytes 20971522 | tf_op jit(solution)/shard_map/dynamic_update_slice | solution.py:62
  331.1 2.0 subtract_reduce_fusion.3
  333.1 7.6 fusion.23
  340.7 12.0 %fusion.10 = f32[16,256,2,256,1]{3,0,4,2,1:T(8,128)} fusion(f32[2,16,256,256,1]{2,3,0,1,4:T(8,128)S(1)} %fusion.23, f32[2,256,2,256]{3,1,2,0:T(8,128)S(1)} %pad_maximum_fusion), kind=kOutput, calls=%fused_computation.12 | convolution fusion | flops 6442450944 | bytes 17825792 | tf_op jit(solution)/shard_map/QjPb,Pabk->Qkaj/dot_general | solution.py:35
  352.7 86.2 %all-to-all-done.3 = f32[16,2,16,16,256]{4,3,1,2,0:T(8,128)} async-done(((f32[16,2,16,16,256]{4,3,1,2,0:T(8,128)}), f32[16,2,16,16,256]{4,3,1,2,0:T(8,128)}, u32[]{:S(2)}, u32[]{:S(2)}) %all-to-all-start.3) | async-done | bytes 8388640 | tf_op jit(solution)/shard_map/all_to_all | solution.py:81
  438.9 39.5 %all-to-all-start.4 = ((f32[16,2,16,16,256]{4,3,1,2,0:T(8,128)}), f32[16,2,16,16,256]{4,3,1,2,0:T(8,128)}, u32[]{:S(2)}, u32[]{:S(2)}) async-start(f32[16,2,16,16,256]{4,3,1,2,0:T(8,128)} %bitcast.252), calls=%async_computation.4 | async-start | bytes 16777216 | tf_op jit(solution)/shard_map/all_to_all | solution.py:81
  478.5 4.0 copy.195
  482.5 12.7 %fusion.4 = f32[16,256,2,256,1,1]{3,1,4,0,2,5:T(8,128)S(1)} fusion(f32[16,2,16,16,256]{4,3,1,2,0:T(8,128)} %all-to-all-done.3, f32[1,256,1,16,16]{1,4,2,0,3:T(8,128)S(1)} %copy-done.7, f32[1,256,1,16,16]{1,4,2,0,3:T(8,128)S(1)} %copy-done.6, f32[1,256,1,16,16]{1,4,2,0,3:T(8,128)S(1)} %copy-done.8), kind=kOutput, calls=%fused_computation.6 | convolution fusion | flops 6443237376 | bytes 17563648 | tf_op jit(solution)/shard_map/RiQsa,sQkaj->Rkij/dot_general | solution.py:43
  495.2 4.0 copy.193
  499.1 2.7 bitcast_dynamic-update-slice_fusion.2
  501.9 5.2 subtract_reduce_fusion.2
  507.1 7.6 fusion.21
  514.7 11.9 %fusion.8 = f32[16,256,2,256,1]{3,0,4,2,1:T(8,128)} fusion(f32[2,16,256,256,1]{2,3,0,1,4:T(8,128)S(1)} %fusion.21, f32[2,256,2,256]{3,1,2,0:T(8,128)S(1)} %pad_maximum_fusion), kind=kOutput, calls=%fused_computation.10 | convolution fusion | flops 6442450944 | bytes 17825792 | tf_op jit(solution)/shard_map/QjPb,Pabk->Qkaj/dot_general | solution.py:35
  526.6 103.6 %all-to-all-done.4 = f32[16,2,16,16,256]{4,3,1,2,0:T(8,128)} async-done(((f32[16,2,16,16,256]{4,3,1,2,0:T(8,128)}), f32[16,2,16,16,256]{4,3,1,2,0:T(8,128)}, u32[]{:S(2)}, u32[]{:S(2)}) %all-to-all-start.4) | async-done | bytes 8388640 | tf_op jit(solution)/shard_map/all_to_all | solution.py:81
  630.2 37.4 %all-to-all-start.5 = ((f32[16,2,16,16,256]{4,3,1,2,0:T(8,128)}), f32[16,2,16,16,256]{4,3,1,2,0:T(8,128)}, u32[]{:S(2)}, u32[]{:S(2)}) async-start(f32[16,2,16,16,256]{4,3,1,2,0:T(8,128)} %bitcast.253), calls=%async_computation.5 | async-start | bytes 16777216 | tf_op jit(solution)/shard_map/all_to_all | solution.py:81
  667.6 2.0 squeeze.48
  669.5 0.6 stack.131
  670.2 2.5 copy.113
  672.7 1.0 copy.114
  673.7 9.6 %fusion.2 = f32[16,256,2,256,1,1]{3,1,4,0,2,5:T(8,128)S(1)} fusion(f32[16,2,16,16,256]{4,3,1,2,0:T(8,128)} %all-to-all-done.4, f32[1,256,1,16,16]{1,4,2,0,3:T(8,128)S(1)} %copy.114, f32[1,256,1,16,16]{1,4,2,0,3:T(8,128)S(1)} %copy.113, f32[1,256,1,16,16]{1,4,2,0,3:T(8,128)S(1)} %neg.37), kind=kOutput, calls=%fused_computation.4 | convolution fusion | flops 6443237376 | bytes 17563648 | tf_op jit(solution)/shard_map/RiQsa,sQkaj->Rkij/dot_general | solution.py:43
  683.4 0.9 copy.192
  684.2 2.6 copy-done.1
  686.9 4.7 add_reduce_fusion.1
  691.6 129.8 %all-to-all-done.5 = f32[16,2,16,16,256]{4,3,1,2,0:T(8,128)} async-done(((f32[16,2,16,16,256]{4,3,1,2,0:T(8,128)}), f32[16,2,16,16,256]{4,3,1,2,0:T(8,128)}, u32[]{:S(2)}, u32[]{:S(2)}) %all-to-all-start.5) | async-done | bytes 8388640 | tf_op jit(solution)/shard_map/all_to_all | solution.py:81
  821.3 9.9 %fusion = f32[16,256,2,256,1,1]{3,1,4,0,2,5:T(8,128)S(1)} fusion(f32[16,2,16,16,256]{4,3,1,2,0:T(8,128)} %all-to-all-done.5, f32[1,256,1,16,16]{1,4,2,0,3:T(8,128)S(1)} %copy.114, f32[1,256,1,16,16]{1,4,2,0,3:T(8,128)S(1)} %copy.113, f32[1,256,1,16,16]{1,4,2,0,3:T(8,128)S(1)} %neg.37), kind=kOutput, calls=%fused_computation.2 | convolution fusion | flops 6443237376 | bytes 17563648 | tf_op jit(solution)/shard_map/RiQsa,sQkaj->Rkij/dot_general | solution.py:43
  831.2 0.9 copy.191
  832.1 2.6 copy-done.2
  834.7 4.7 add_reduce_fusion
  839.4 1.3 maximum_bitcast_fusion.17
  840.7 1.3 maximum_bitcast_fusion.18
  842.1 1.3 maximum_bitcast_fusion.19
  843.4 1.3 maximum_bitcast_fusion.20
  844.8 0.6 broadcast_in_dim.32
  845.4 39.1 %all-to-all-start.6 = ((f32[16,1,8]{2,1,0:T(1,128)}), f32[16,1,8]{2,1,0:T(1,128)S(1)}, u32[]{:S(2)}, u32[]{:S(2)}) async-start(f32[16,1,8]{2,1,0:T(1,128)} %broadcast_in_dim.32), calls=%async_computation.6 | async-start | bytes 16384 | tf_op jit(solution)/shard_map/all_to_all | solution.py:92
  884.6 6.2 bitcast_dynamic-update-slice_fusion.1
  890.8 1.0 copy-done.3
  891.9 2.5 bitcast_dynamic-update-slice_fusion
  894.4 21.6 %copy.119 = bf16[2,2,2,16,256,256]{5,4,3,2,1,0:T(8,128)(2,1)} copy(bf16[2,2,2,16,256,256]{4,5,0,3,2,1:T(8,128)(2,1)} %bitcast_dynamic-update-slice_fusion) | data formatting | bytes 33554432
  916.0 0.7 mul.87
  (50 shorter events, 1.2 us)
Async XLA Ops:
  0.6 29.7 %copy-start.9 = (s32[2]{0:T(128)S(1)}, s32[2]{0:T(128)}, u32[]{:S(2)}) copy-start(s32[2]{0:T(128)} %param.7) | copy-start | bytes 28
  2.8 23.5 %all-to-all-start = ((f32[16,2,16,256]{3,2,1,0:T(8,128)}), f32[16,2,16,256]{3,2,1,0:T(8,128)S(1)}, u32[]{:S(2)}, u32[]{:S(2)}) async-start(f32[16,2,16,256]{3,2,1,0:T(8,128)} %dynamic-slice_bitcast_fusion), calls=%async_computation | async-start | bytes 1048576 | tf_op jit(solution)/shard_map/all_to_all | solution.py:19
  27.4 31.2 %all-to-all-start.1 = ((f32[32,2,16,256]{3,2,1,0:T(8,128)}), f32[32,2,16,256]{3,2,1,0:T(8,128)S(1)}, u32[]{:S(2)}, u32[]{:S(2)}) async-start(f32[32,2,16,256]{3,2,1,0:T(8,128)} %broadcast_in_dim.26), calls=%async_computation.1 | async-start | bytes 2097152 | tf_op jit(solution)/shard_map/all_to_all | solution.py:24
  80.2 166.1 %all-to-all-start.2 = ((f32[16,2,16,16,256]{4,3,1,2,0:T(8,128)}), f32[16,2,16,16,256]{4,3,1,2,0:T(8,128)}, u32[]{:S(2)}, u32[]{:S(2)}) async-start(f32[16,2,16,16,256]{4,3,1,2,0:T(8,128)} %bitcast.254), calls=%async_computation.2 | async-start | bytes 16777216 | tf_op jit(solution)/shard_map/all_to_all | solution.py:81
  246.3 192.6 %all-to-all-start.3 = ((f32[16,2,16,16,256]{4,3,1,2,0:T(8,128)}), f32[16,2,16,16,256]{4,3,1,2,0:T(8,128)}, u32[]{:S(2)}, u32[]{:S(2)}) async-start(f32[16,2,16,16,256]{4,3,1,2,0:T(8,128)} %bitcast.251), calls=%async_computation.3 | async-start | bytes 16777216 | tf_op jit(solution)/shard_map/all_to_all | solution.py:81
  297.0 2.6 copy-start.5
  310.8 3.2 copy-start.4
  315.0 16.1 %slice-start.4 = ((s8[8388608]{0:T(1024)(128)(4,1)}), s8[4194304]{0:T(1024)(128)(4,1)S(1)}, s32[]{:S(2)}) async-start(s8[8388608]{0:T(1024)(128)(4,1)} %bitcast.246), calls=%async_computation.11 | async-start | bytes 8388608
  315.0 18.1 %slice-start.2 = ((s8[8388608]{0:T(1024)(128)(4,1)}), s8[4194304]{0:T(1024)(128)(4,1)S(1)}, s32[]{:S(2)}) async-start(s8[8388608]{0:T(1024)(128)(4,1)} %bitcast.243), calls=%async_computation.9 | async-start | bytes 8388608
  321.2 9.9 %slice-start.5 = ((s8[8388608]{0:T(1024)(128)(4,1)}), s8[4194304]{0:T(1024)(128)(4,1)S(1)}, s32[]{:S(2)}) async-start(s8[8388608]{0:T(1024)(128)(4,1)} %bitcast.246), calls=%async_computation.12 | async-start | bytes 8388608
  321.2 11.9 %slice-start.3 = ((s8[8388608]{0:T(1024)(128)(4,1)}), s8[4194304]{0:T(1024)(128)(4,1)S(1)}, s32[]{:S(2)}) async-start(s8[8388608]{0:T(1024)(128)(4,1)} %bitcast.243), calls=%async_computation.10 | async-start | bytes 8388608
  438.9 191.3 %all-to-all-start.4 = ((f32[16,2,16,16,256]{4,3,1,2,0:T(8,128)}), f32[16,2,16,16,256]{4,3,1,2,0:T(8,128)}, u32[]{:S(2)}, u32[]{:S(2)}) async-start(f32[16,2,16,16,256]{4,3,1,2,0:T(8,128)} %bitcast.252), calls=%async_computation.4 | async-start | bytes 16777216 | tf_op jit(solution)/shard_map/all_to_all | solution.py:81
  478.4 4.0 copy-start.6
  478.4 4.0 copy-start.7
  478.4 4.0 copy-start.8
  482.5 19.4 %copy-start = (f32[2,1,16,256,256]{4,3,0,2,1:T(8,128)}, f32[2,1,16,256,256]{4,3,0,2,1:T(8,128)S(1)}, u32[]{:S(2)}) copy-start(f32[2,1,16,256,256]{4,3,0,2,1:T(8,128)S(1)} %copy.195) | copy-start | bytes 25165828
  499.1 7.9 slice-start
  501.9 5.2 slice-start.1
  630.2 191.2 %all-to-all-start.5 = ((f32[16,2,16,16,256]{4,3,1,2,0:T(8,128)}), f32[16,2,16,16,256]{4,3,1,2,0:T(8,128)}, u32[]{:S(2)}, u32[]{:S(2)}) async-start(f32[16,2,16,16,256]{4,3,1,2,0:T(8,128)} %bitcast.253), calls=%async_computation.5 | async-start | bytes 16777216 | tf_op jit(solution)/shard_map/all_to_all | solution.py:81
  683.3 3.5 copy-start.1
  831.2 3.5 copy-start.2
  845.4 70.5 %all-to-all-start.6 = ((f32[16,1,8]{2,1,0:T(1,128)}), f32[16,1,8]{2,1,0:T(1,128)S(1)}, u32[]{:S(2)}, u32[]{:S(2)}) async-start(f32[16,1,8]{2,1,0:T(1,128)} %broadcast_in_dim.32), calls=%async_computation.6 | async-start | bytes 16384 | tf_op jit(solution)/shard_map/all_to_all | solution.py:92
  884.6 7.3 copy-start.3
